TPU v7x, 32 devices: a whole 2x2x4 slice. The times are simulated.
32 devices in a mesh: group: 4 (over y, core), tile: 8 (over z, x).
Axes of the slice: x: 2, y: 2, z: 4, core: 2. Of those that a mesh axis runs over, the one named last changes fastest.
Arguments:
- embeddings: bfloat16 [12288, 768], P(('group', 'tile')), may hold values from -15 to 15
- clusters: int32 [12288], P(('group', 'tile')), may hold values from 0 to 15, as said below
- cluster_owner: int32 [16], replicated, may hold values from 0 to 3, as said below
Outputs:
- neighbours: bfloat16 [12288, 768], P(('group', 'tile'))
- log_mass: float32 [12288], P(('group', 'tile'))
Inputs may be any that keep to these rules, and one draw needn't show every extreme that they name: Among the 384 rows of one device at most 144 belong to clusters of any one group; in every draw one group has exactly 144 rows on every device. `cluster_owner`: each group owns exactly 4 clusters.
All inputs are finite; a program needn't handle non-finite values.
Results may differ from a plain program's by a relative error of at most 0.034.
Values may be sent and summed in bfloat16 or wider, within the bound.
A program may use at most 128 MiB of HBM per device.

v0:
```python
import math

import jax
import jax.numpy as jnp
from jax import lax
from jax.sharding import PartitionSpec as P

score_scale = 3.0
penalty = 2.0


def block_scores(queries, query_ids, key_rows, key_ids):
    feature_width = queries.shape[1]
    products = lax.dot_general(
        queries, key_rows, (((1,), (1,)), ((), ())), preferred_element_type=jnp.float32
    )
    differs = (query_ids[:, None] != key_ids[None, :]).astype(jnp.float32)
    return products * (score_scale / math.sqrt(feature_width)) - penalty * differs


def partial_terms(scores, usable, key_rows):
    row_peak = jnp.max(jnp.where(usable, scores, 0.0), axis=1)
    weights = jnp.exp(jnp.where(usable, scores - row_peak[:, None], -jnp.inf))
    row_total = jnp.sum(weights, axis=1)
    weighted = jnp.dot(weights.astype(jnp.bfloat16), key_rows, preferred_element_type=jnp.float32)
    return (row_peak, row_total, weighted)


def combine_terms(former, second):
    row_peak = jnp.maximum(former[0], second[0])
    factor_one = jnp.exp(former[0] - row_peak)
    factor_two = jnp.exp(second[0] - row_peak)
    row_total = former[1] * factor_one + second[1] * factor_two
    weighted = second[2] * factor_two[:, None]
    return (row_peak, row_total, weighted)


def per_device(embeddings, clusters, cluster_owner):
    row_count = embeddings.shape[0]
    feature_width = embeddings.shape[1]
    groups_total = lax.axis_size("group")
    capacity = 3 * row_count // (2 * groups_total)
    slot_count = groups_total * capacity
    cluster_total = cluster_owner.shape[0]
    table_hit = clusters[:, None] == jnp.arange(cluster_total, dtype=jnp.int32)[None, :]
    group_of = jnp.sum(jnp.where(table_hit, cluster_owner[None, :], 0), axis=1)
    same_group = group_of[:, None] == group_of[None, :]
    row_index = jnp.arange(row_count, dtype=jnp.int32)
    earlier = row_index[None, :] < row_index[:, None]
    rank_in = jnp.sum(same_group & earlier, axis=1)
    slot_of = group_of * capacity + rank_in
    slot_index = jnp.arange(slot_count, dtype=jnp.int32)
    placing = slot_index[:, None] == slot_of[None, :]
    outgoing = jnp.dot(
        placing.astype(jnp.bfloat16), embeddings, preferred_element_type=jnp.float32
    ).astype(jnp.bfloat16)
    outgoing_ids = jnp.sum(jnp.where(placing, clusters[None, :] + 1, 0), axis=1) - 1
    arrived, arrived_ids = (
        lax.all_to_all(
            outgoing.reshape(groups_total, capacity, feature_width),
            "group",
            split_axis=0,
            concat_axis=0,
            tiled=True,
        ),
        lax.all_to_all(
            outgoing_ids.reshape(groups_total, capacity),
            "group",
            split_axis=0,
            concat_axis=0,
            tiled=True,
        ),
    )
    queries = arrived.reshape(slot_count, feature_width)
    query_ids = arrived_ids.reshape(slot_count)
    start_state = (
        jnp.zeros((slot_count,), jnp.float32),
        jnp.ones((slot_count,), jnp.float32),
        jnp.zeros((slot_count, feature_width), jnp.float32),
    )
    tile_pos = lax.axis_index("tile")
    query_pos = tile_pos * slot_count + jnp.arange(slot_count, dtype=jnp.int32)
    key_rows = lax.all_gather(queries, "tile", axis=0, tiled=True)
    key_ids = lax.all_gather(query_ids, "tile", axis=0, tiled=True)
    key_pos = jnp.arange(key_rows.shape[0], dtype=jnp.int32)
    scores = block_scores(queries, query_ids, key_rows, key_ids)
    usable = (key_ids[None, :] >= 0) & (key_pos[None, :] != query_pos[:, None])
    partials = combine_terms(start_state, partial_terms(scores, usable, key_rows))
    row_peak, row_total, weighted = partials
    lse_slots = row_peak + jnp.log(row_total)
    neighbour_slots = (weighted / row_total[:, None]).astype(jnp.bfloat16)
    back_rows, back_lse = (
        lax.all_to_all(
            neighbour_slots.reshape(groups_total, capacity, feature_width),
            "group",
            split_axis=0,
            concat_axis=0,
            tiled=True,
        ),
        lax.all_to_all(
            lse_slots.reshape(groups_total, capacity).astype(jnp.bfloat16),
            "group",
            split_axis=0,
            concat_axis=0,
            tiled=True,
        ).astype(jnp.float32),
    )
    flat_rows = back_rows.reshape(slot_count, feature_width)
    neighbours = jnp.take(flat_rows, slot_of, axis=0)
    log_mass = jnp.take(back_lse.reshape(slot_count), slot_of, axis=0).astype(jnp.float32)
    return (neighbours, log_mass)


def solution(mesh):
    placed = (P(("group", "tile"), None), P(("group", "tile")), P())
    return jax.shard_map(
        per_device,
        mesh=mesh,
        in_specs=placed,
        out_specs=(P(("group", "tile"), None), P(("group", "tile"))),
        check_vma=False,
    )
```

profile of v0, /device:TPU:0, one launch (start us, length us, event | category | flops | bytes accessed | tf_op | source)
XLA Modules:
  0.0 201.2 jit_solution(10682576247916867864)
XLA Ops:
  7.2 0.8 select_reduce_fusion.2
  8.1 0.2 convert_reduce_fusion
  8.3 0.7 multiply_add_fusion
  9.0 0.6 convolution_convert_fusion
  9.6 16.9 %all_to_all.22 = bf16[4,144,768]{2,1,0:T(8,128)(2,1)} all-to-all(bf16[4,144,768]{2,1,0:T(8,128)(2,1)S(1)} %bitcast.12), channel_id=1, replica_groups=mesh['group'=4,'tile'=8] {'group'}, dimensions={0} | all-to-all | bytes 1769472 | tf_op jit(solution)/shard_map/all_to_all | solution.py:59
  26.5 0.2 select_reduce_fusion.1
  26.7 0.7 sub.55
  27.3 3.2 %all-to-all-start = ((s32[4,1,144]{2,1,0:T(1,128)}), s32[4,1,144]{2,1,0:T(1,128)S(1)}, u32[]{:S(2)}, u32[]{:S(2)}) async-start(s32[4,1,144]{2,1,0:T(1,128)} %sub.55), calls=%async_computation | async-start | bytes 8192 | tf_op jit(solution)/shard_map/all_to_all | solution.py:66
  30.6 1.2 dynamic-slice
  32.5 1.8 all-to-all-done
  34.5 0.3 dynamic-update-slice
  34.8 38.7 %all-reduce = s32[4608]{0:T(1024)S(1)} all-reduce(s32[4608]{0:T(1024)S(1)} %dynamic-update-slice), channel_id=1, replica_groups=mesh['group'=4,'tile'=8] {'tile'}, use_global_device_ids=true, to_apply=%add | all-reduce | flops 4608 | bytes 36864
  73.5 63.3 %all-gather.2.cloned.1.call-done = bf16[4608,768]{1,0:T(8,128)(2,1)} async-done(((bf16[576,768]{1,0:T(8,128)(2,1)}), bf16[4608,768]{1,0:T(8,128)(2,1)}) %all-gather.2.cloned.1.call-update) | async-done | bytes 7077904 | tf_op jit(solution)/shard_map/all_gather | solution.py:83
  136.8 12.9 %select_reduce_fusion = (f32[576]{0:T(1024)S(1)}, f32[576,4608]{1,0:T(8,128)}) fusion(s32[576]{0:T(1024)S(1)} %iota_add_fusion, pred[4608]{0:T(1024)(128)(4,1)S(1)} %broadcast_compare_fusion, s32[4608]{0:T(1024)S(1)} %all-reduce, s32[576]{0:T(1024)S(1)} %reshape.184, bf16[576,768]{1,0:T(8,128)(2,1)} %bitcast.11, ...), kind=kOutput, calls=%fused_computation.3 | convolution fusion | flops 4098096640 | bytes 18609408 | tf_op jit(solution)/shard_map/dot_general | solution.py:14
  149.8 7.8 %fusion.1 = f32[576]{0:T(1024)S(1)} fusion(f32[576,4608]{1,0:T(8,128)} %get-tuple-element.7, f32[576]{0:T(1024)S(1)} %get-tuple-element.6, s32[576]{0:T(1024)S(1)} %iota_add_fusion, pred[4608]{0:T(1024)(128)(4,1)S(1)} %broadcast_compare_fusion), kind=kLoop, calls=%fused_computation.7 | loop fusion | flops 13270464 | bytes 10628352 | tf_op jit(solution)/shard_map/reduce_sum | solution.py:24
  157.8 0.6 copy.5
  158.4 3.4 %all-to-all-start.3 = ((bf16[4,1,144]{2,1,0:T(2,128)(2,1)}), bf16[4,1,144]{2,1,0:T(2,128)(2,1)S(1)}, u32[]{:S(2)}, u32[]{:S(2)}) async-start(bf16[4,1,144]{2,1,0:T(2,128)(2,1)} %copy.5), calls=%async_computation.3 | async-start | bytes 8192 | tf_op jit(solution)/shard_map/all_to_all | solution.py:100
  161.8 13.2 %divide_convert_fusion = bf16[576,768]{1,0:T(8,128)(2,1)} fusion(bf16[4608,768]{1,0:T(8,128)(2,1)} %all-gather.2.cloned.1.call-done, f32[576,4608]{1,0:T(8,128)} %get-tuple-element.7, f32[576]{0:T(1024)S(1)} %get-tuple-element.6, s32[576]{0:T(1024)S(1)} %iota_add_fusion, pred[4608]{0:T(1024)(128)(4,1)S(1)} %broadcast_compare_fusion, ...), kind=kOutput, calls=%fused_computation.14 | convolution fusion | flops 4091461632 | bytes 18593280 | tf_op jit(solution)/shard_map/dot_general | solution.py:25
  175.0 3.5 %all-to-all-start.2 = ((bf16[4,144,768]{2,1,0:T(8,128)(2,1)}), bf16[4,144,768]{2,1,0:T(8,128)(2,1)S(1)}, u32[]{:S(2)}, u32[]{:S(2)}) async-start(bf16[4,144,768]{2,1,0:T(8,128)(2,1)} %bitcast.3), calls=%async_computation.2 | async-start | bytes 1769472 | tf_op jit(solution)/shard_map/all_to_all | solution.py:93
  178.7 1.9 gather_fusion.1
  180.6 0.6 broadcast_select_fusion.1
  181.1 10.1 %all-to-all-done.2 = bf16[4,144,768]{2,1,0:T(8,128)(2,1)S(1)} async-done(((bf16[4,144,768]{2,1,0:T(8,128)(2,1)}), bf16[4,144,768]{2,1,0:T(8,128)(2,1)S(1)}, u32[]{:S(2)}, u32[]{:S(2)}) %all-to-all-start.2) | async-done | bytes 884768 | tf_op jit(solution)/shard_map/all_to_all | solution.py:93
  191.2 2.2 %gather_fusion = bf16[384,768]{1,0:T(8,128)(2,1)S(1)} fusion(bf16[576,768]{1,0:T(8,128)(2,1)S(1)} %bitcast.9, s32[1024]{0:T(1024)S(1)} %pad_clamp_fusion), kind=kCustom, calls=%fused_computation | custom fusion | bytes 1181184 | tf_op jit(solution)/shard_map/jit(_take)/gather | solution.py:109
  193.4 0.9 broadcast_select_fusion
  (19 shorter events, 0.5 us)
Async XLA Ops:
  7.2 1.8 copy-start
  7.2 129.7 %all-gather.2.cloned.1.call-start = ((), (), s32[]{:S(2)}) async-start(), calls=%async_computation.4 | async-start | bytes 7962624 | tf_op jit(solution)/shard_map/all_gather | solution.py:83
  27.3 7.0 %all-to-all-start = ((s32[4,1,144]{2,1,0:T(1,128)}), s32[4,1,144]{2,1,0:T(1,128)S(1)}, u32[]{:S(2)}, u32[]{:S(2)}) async-start(s32[4,1,144]{2,1,0:T(1,128)} %sub.55), calls=%async_computation | async-start | bytes 8192 | tf_op jit(solution)/shard_map/all_to_all | solution.py:66
  158.4 16.6 %all-to-all-start.3 = ((bf16[4,1,144]{2,1,0:T(2,128)(2,1)}), bf16[4,1,144]{2,1,0:T(2,128)(2,1)S(1)}, u32[]{:S(2)}, u32[]{:S(2)}) async-start(bf16[4,1,144]{2,1,0:T(2,128)(2,1)} %copy.5), calls=%async_computation.3 | async-start | bytes 8192 | tf_op jit(solution)/shard_map/all_to_all | solution.py:100
  175.0 16.2 %all-to-all-start.2 = ((bf16[4,144,768]{2,1,0:T(8,128)(2,1)}), bf16[4,144,768]{2,1,0:T(8,128)(2,1)S(1)}, u32[]{:S(2)}, u32[]{:S(2)}) async-start(bf16[4,144,768]{2,1,0:T(8,128)(2,1)} %bitcast.3), calls=%async_computation.2 | async-start | bytes 1769472 | tf_op jit(solution)/shard_map/all_to_all | solution.py:93
Sparse Core Ops, SparseCore 0:
  26.6 110.1 all-gather.1
where the time goes:
time: 202 us; the launch traced here: 201 us
  waiting for transfers between devices  75.3 us (37%)
  blocking collectives  55.6 us (28%)
  matrix products  26.7 us (13%)
  between operations  14.8 us (7%)
  other arithmetic  11.4 us (6%)
  starting transfers between devices  10.2 us (5%)
  local copies, waits for them, and re-layouts  7.19 us (4%)
    all_gather x1, waiting for transfers between devices, per_device(): key_rows = lax.all_gather(queries, 'tile', axis=0, tiled=True)  63.3 us
    unnamed x1, blocking collectives  38.7 us
    all_to_all x1, blocking collectives, per_device(): lax.all_to_all(outgoing.reshape(groups_total, capacity, feature_width), '...  16.9 us
    dot_general x1, matrix products, partial_terms(): jnp.dot(weights.astype(jnp.bfloat16), key_rows, preferred_element_type=jn...  13.2 us
    dot_general x1, matrix products, block_scores(): lax.dot_general(queries, key_rows, (((1,), (1,)), ((), ())), preferred_el...  12.9 us
    all_to_all x1, waiting for transfers between devices, per_device(): lax.all_to_all(neighbour_slots.reshape(groups_total, capacity, feature_wi...  10.1 us
    reduce_sum x1, other arithmetic, partial_terms(): row_total = jnp.sum(weights, axis=1)  7.8 us
  transfers between devices with their start and end apart: 4, of which 3 were waited for; matrix products, arithmetic and copies ran while one was open for 9% of the time, Pallas kernels for 0%

commit v1 on v0

v1 whole, which is shorter than its diff:
```python
import functools
import math

import jax
import jax.numpy as jnp
from jax import lax
from jax.experimental import pallas as pl
from jax.experimental.pallas import tpu as pltpu
from jax.sharding import PartitionSpec as P

MESH = pl.DeviceIdType.MESH
score_scale = 3.0
penalty = 2.0
LOG2E = math.log2(math.e)
LN2 = math.log(2.0)
NEVER = -1e30
SUB = 2


def iota(shape, dim):
    return lax.broadcasted_iota(jnp.int32, shape, dim)


def kernel(
    planes, group_size, cap, lanes, emb_ref, clusters_ref, owner_ref, out_ref, mass_ref,
    keys, ids, queries, query_ids, acc, peak, total, outgoing, out_ids, results, masses, back, back_mass,
    send_sem, recv_sem,
):
    rows, width = emb_ref.shape
    ys = group_size // 2
    members = group_size * SUB
    group_pos = lax.axis_index("group")
    tile_pos = lax.axis_index("tile")
    my_y, my_core = group_pos // 2, group_pos % 2
    my_plane, my_sub = tile_pos // SUB, tile_pos % SUB

    def member(dy, dc, ds):
        return (dy * 2 + dc) * SUB + ds

    def peer(dy, dc, ds):
        y = lax.rem(my_y + dy, ys)
        core = 1 - my_core if dc else my_core
        sub = 1 - my_sub if ds else my_sub
        return (y * 2 + core, my_plane * SUB + sub)

    def plane_of(r):
        place = 0
        bit = 1
        while bit < planes:
            mine = (my_plane // bit) % 2
            place = place + (1 - mine if r & bit else mine) * bit
            bit *= 2
        return place

    def far(r):
        return (group_pos, plane_of(r) * SUB + my_sub)

    everyone = [(dy, dc, ds) for dy in range(ys) for dc in range(2) for ds in range(SUB)][1:]

    barrier = pltpu.get_barrier_semaphore()
    for offset in everyone:
        pl.semaphore_signal(barrier, inc=1, device_id=peer(*offset), device_id_type=MESH)
    for r in range(1, planes):
        pl.semaphore_signal(barrier, inc=1, device_id=far(r), device_id_type=MESH)

    clusters = clusters_ref[...]
    group_row = jnp.zeros_like(clusters)
    for c in range(owner_ref.shape[0]):
        group_row = jnp.where(clusters == c, owner_ref[c], group_row)
    group_row = group_row ^ my_plane
    eye = iota((rows, rows), 0) == iota((rows, rows), 1)
    before = iota((rows, rows), 0) < iota((rows, rows), 1)

    def column(row):
        return jnp.sum(jnp.where(eye, row, 0), axis=1, keepdims=True)

    group_col = column(group_row)
    rank_row = jnp.sum(((group_col == group_row) & before).astype(jnp.int32), axis=0, keepdims=True)
    slot_row = group_row * cap + rank_row
    slot_col = column(slot_row)
    cluster_col = column(clusters)
    placing = (iota((planes * cap, rows), 0) == slot_row).astype(jnp.bfloat16)
    placed = jnp.dot(placing, emb_ref[...], preferred_element_type=jnp.float32).astype(jnp.bfloat16)
    outgoing[...] = placed.reshape(planes, cap, width)
    keys[0, 0] = placed[:cap]
    for r in range(planes):
        lane = iota((rows, lanes), 1)
        here = (lane + r * cap == slot_col) & (lane < cap)
        row = jnp.sum(jnp.where(here, cluster_col + 1, 0), axis=0, keepdims=True) - 1
        out_ids[r] = row
        if r == 0:
            ids[0, 0] = row

    pl.semaphore_wait(barrier, len(everyone) + planes - 1)

    copies = []

    def send(src, dst, to):
        index = len(copies)
        copy = pltpu.make_async_remote_copy(
            src_ref=src, dst_ref=dst, send_sem=send_sem.at[index], recv_sem=recv_sem.at[index],
            device_id=to, device_id_type=MESH,
        )
        copy.start()
        copies.append(copy)
        return copy

    half = (cap // 32 + (1 if cap % 32 else 0)) * 16
    lower, upper = pl.ds(0, half), pl.ds(half, cap - half)

    id_far = [None] + [send(out_ids.at[r], ids.at[0, r], far(r)) for r in range(1, planes)]
    row_far = [None] + [send(outgoing.at[r], keys.at[r, 0], far(r)) for r in range(1, planes)]

    across, along = {}, {}
    last = {r: [] for r in range(planes)}

    def own(r):
        if r:
            row_far[r].wait_recv()
        mine = keys.at[r, 0]
        across[r] = send(mine, keys.at[r, member(0, 0, 1)], peer(0, 0, 1))
        along[r] = [
            send(mine, keys.at[r, member(ys - d, 0, 0)], peer(d, 0, 0)) for d in range(1, ys)
        ]
        last[r].append(send(mine, keys.at[r, member(0, 1, 0)], peer(0, 1, 0)))
        first = (planes - 1 - r) * cap
        queries[first:first + cap, :] = mine[...]

    diagonal = {}

    def forward(r):
        across[r].wait_recv()
        side = keys.at[r, member(0, 0, 1)]
        turned = [
            send(side.at[lower], keys.at[r, member(ys - d, 0, 1)].at[lower], peer(d, 0, 0))
            for d in range(1, ys)
        ]
        last[r].append(send(side, keys.at[r, member(0, 1, 1)], peer(0, 1, 0)))
        crossed = []
        for d in range(1, ys):
            along[r][d - 1].wait_recv()
            side = keys.at[r, member(ys - d, 0, 0)]
            crossed.append(
                send(side.at[upper], keys.at[r, member(ys - d, 0, 1)].at[upper], peer(0, 0, 1))
            )
            last[r].append(send(side, keys.at[r, member(ys - d, 1, 0)], peer(0, 1, 0)))
        diagonal[r] = turned + crossed

    def share(r):
        for copy in diagonal[r]:
            copy.wait_recv()
        for d in range(1, ys):
            last[r].append(
                send(keys.at[r, member(ys - d, 0, 1)], keys.at[r, member(ys - d, 1, 1)], peer(0, 1, 0))
            )

    own(0)
    for r in range(1, planes):
        id_far[r].wait_recv()
    id_near = [
        send(ids.at[0], ids.at[member((ys - dy) % ys, dc, ds)], peer(dy, dc, ds))
        for dy, dc, ds in everyone
    ]
    for r in range(1, planes):
        own(r)
        forward(r - 1)
        if r > 1:
            share(r - 2)

    part = planes * cap // 2
    for r in range(planes):
        first = (planes - 1 - r) * cap
        pick = iota((cap, lanes), 0) == iota((cap, lanes), 1)
        query_ids[first:first + cap, :] = jnp.sum(
            jnp.where(pick, ids[0, r], 0), axis=1, keepdims=True
        )
    acc[...] = jnp.zeros_like(acc)
    peak[...] = jnp.zeros_like(peak)
    total[...] = jnp.ones_like(total)
    for copy in id_near:
        copy.wait_recv()

    def step(r, h):
        start = h * part
        if not isinstance(start, int):
            start = pl.multiple_of(start, 16)
        mine = pl.ds(start, part)
        block = keys[r].reshape(members * cap, width)
        scores = lax.dot_general(
            queries[mine, :], block, (((1,), (1,)), ((), ())), preferred_element_type=jnp.float32
        )
        key_ids = jnp.concatenate([ids[p, r][:, :cap] for p in range(members)], axis=1)
        other = jnp.where(key_ids < 0, NEVER, -penalty * LOG2E)
        bias = jnp.where(query_ids[mine, :] == key_ids, 0.0, other)
        scores = scores * (score_scale * LOG2E / math.sqrt(width)) + bias
        head = scores[:, :lanes]
        lane = iota((part, lanes), 1)
        itself = (iota((part, lanes), 0) - ((planes - 1 - r) * cap - start) == lane) & (lane < cap)
        scores = jnp.concatenate([jnp.where(itself, NEVER, head), scores[:, lanes:]], axis=1)
        old = peak[mine, :]
        new = jnp.maximum(old, jnp.max(scores, axis=1, keepdims=True))
        shrink = jnp.exp2(old - new)
        weights = jnp.exp2(scores - new)
        total[mine, :] = total[mine, :] * shrink + jnp.sum(weights, axis=1, keepdims=True)
        peak[mine, :] = new
        acc[mine, :] = acc[mine, :] * shrink + jnp.dot(
            weights.astype(jnp.bfloat16), block, preferred_element_type=jnp.float32
        )

    def both(r):
        def body(h, carry):
            step(r, h)
            return carry

        lax.fori_loop(0, 2, body, 0)

    def finish(r):
        for copy in last[r]:
            copy.wait_recv()

    for r in range(planes - 2):
        finish(r)
        both(r)
    forward(planes - 1)
    share(planes - 2)
    finish(planes - 2)
    both(planes - 2)
    share(planes - 1)
    finish(planes - 1)

    returned = []
    for h in range(2):
        step(planes - 1, h)
        for spot in range(h * planes // 2, (h + 1) * planes // 2):
            r = planes - 1 - spot
            first = spot * cap
            sums = total[first:first + cap, :]
            results[r] = (acc[first:first + cap, :] / sums).astype(jnp.bfloat16)
            mass = peak[first:first + cap, :] * LN2 + jnp.log(sums)
            pick = iota((cap, lanes), 0) == iota((cap, lanes), 1)
            masses[r] = jnp.sum(jnp.where(pick, mass, 0.0), axis=0, keepdims=True)
            if r:
                returned.append(send(results.at[r], back.at[r], far(r)))
                returned.append(send(masses.at[r], back_mass.at[r], far(r)))
            else:
                back[0] = results[0]
                back_mass[0] = masses[0]
    for copy in returned:
        copy.wait_recv()

    fetch = (iota((rows, planes * cap), 1) == slot_col).astype(jnp.bfloat16)
    found = back[...].reshape(planes * cap, width)
    out_ref[...] = jnp.dot(fetch, found, preferred_element_type=jnp.float32).astype(jnp.bfloat16)
    mass = jnp.zeros((rows, 1), jnp.float32)
    for r in range(planes):
        lane = iota((rows, lanes), 1)
        here = (lane + r * cap == slot_col) & (lane < cap)
        mass = mass + jnp.sum(jnp.where(here, back_mass[r], 0.0), axis=1, keepdims=True)
    mass_ref[...] = jnp.sum(jnp.where(eye, mass, 0.0), axis=0, keepdims=True)
    for copy in copies:
        copy.wait_send()


def per_device(embeddings, clusters, cluster_owner):
    rows, width = embeddings.shape
    group_size = lax.axis_size("group")
    tiles = lax.axis_size("tile")
    planes = tiles // SUB
    assert planes == group_size and planes & (planes - 1) == 0
    most = 3 * rows // (2 * group_size)
    cap = -(-most // 16) * 16
    lanes = -(-cap // 128) * 128
    members = group_size * SUB
    slots = planes * cap
    ys = group_size // 2
    count = 3 * (planes - 1) + planes - 1 + members - 1 + planes * (2 + ys - 1 + 4 * (ys - 1) + 1 + ys)
    vmem = pl.BlockSpec(memory_space=pltpu.VMEM)
    out, mass = pl.pallas_call(
        functools.partial(kernel, planes, group_size, cap, lanes),
        out_shape=(
            jax.ShapeDtypeStruct((rows, width), jnp.bfloat16),
            jax.ShapeDtypeStruct((1, rows), jnp.float32),
        ),
        in_specs=[vmem, vmem, pl.BlockSpec(memory_space=pltpu.SMEM)],
        out_specs=(vmem, vmem),
        scratch_shapes=[
            pltpu.VMEM((planes, members, cap, width), jnp.bfloat16),
            pltpu.VMEM((members, planes, 1, lanes), jnp.int32),
            pltpu.VMEM((slots, width), jnp.bfloat16),
            pltpu.VMEM((slots, 1), jnp.int32),
            pltpu.VMEM((slots, width), jnp.float32),
            pltpu.VMEM((slots, 1), jnp.float32),
            pltpu.VMEM((slots, 1), jnp.float32),
            pltpu.VMEM((planes, cap, width), jnp.bfloat16),
            pltpu.VMEM((planes, 1, lanes), jnp.int32),
            pltpu.VMEM((planes, cap, width), jnp.bfloat16),
            pltpu.VMEM((planes, 1, lanes), jnp.float32),
            pltpu.VMEM((planes, cap, width), jnp.bfloat16),
            pltpu.VMEM((planes, 1, lanes), jnp.float32),
            pltpu.SemaphoreType.DMA((count,)),
            pltpu.SemaphoreType.DMA((count,)),
        ],
        compiler_params=pltpu.CompilerParams(
            collective_id=0, has_side_effects=True, vmem_limit_bytes=48 * 1024 * 1024
        ),
    )(embeddings, clusters.reshape(1, rows), cluster_owner)
    return out, mass.reshape(rows)


def solution(mesh):
    placed = (P(("group", "tile"), None), P(("group", "tile")), P())
    return jax.shard_map(
        per_device,
        mesh=mesh,
        in_specs=placed,
        out_specs=(P(("group", "tile"), None), P(("group", "tile"))),
        check_vma=False,
    )
```

time: 202 us -> 74.9 us (0.37)
  waiting for transfers between devices: 75.3 us -> 0 us
  Pallas kernels: 0 us -> 70.9 us
  blocking collectives: 55.6 us -> 0 us
  matrix products: 26.7 us -> 0 us
  between operations: 14.8 us -> 0.65 us
  other arithmetic: 11.4 us -> 0.6 us
  starting transfers between devices: 10.2 us -> 0 us
  local copies, waits for them, and re-layouts: 7.19 us -> 2.57 us
    pallas_call x0 -> x1, Pallas kernels: none -> 70.9 us  [per_device(): pl.pallas_call(functools.partial(kernel, planes, group_size, cap, lanes),...]
    all_gather x1 -> x0, waiting for transfers between devices: 63.3 us -> none  [per_device(): key_rows = lax.all_gather(queries, 'tile', axis=0, tiled=True)]
    unnamed x1 -> x0, blocking collectives: 38.7 us -> none
    dot_general x3 -> x0, matrix products: 26.7 us -> none  [the longest x1 13.2 us: partial_terms(): jnp.dot(weights.astype(jnp.bfloat16), key_rows, preferred_element_type=jn...]
    all_to_all x1 -> x0, blocking collectives: 16.9 us -> none  [per_device(): lax.all_to_all(outgoing.reshape(groups_total, capacity, feature_width), '...]
    all_to_all x3 -> x0, waiting for transfers between devices: 11.9 us -> none  [the longest x1 10.1 us: per_device(): lax.all_to_all(neighbour_slots.reshape(groups_total, capacity, feature_wi...]
    all_to_all x3 -> x0, starting transfers between devices: 10.2 us -> none  [the longest x1 3.5 us: per_device(): lax.all_to_all(neighbour_slots.reshape(groups_total, capacity, feature_wi...]
    reduce_sum x4 -> x0, other arithmetic: 9.05 us -> none  [the longest x1 7.8 us: partial_terms(): row_total = jnp.sum(weights, axis=1)]
  transfers between devices with their start and end apart: 4 -> 0, of which waited for: 3 -> 0; matrix products, arithmetic and copies ran while one was open for 9% -> 0% of each run, Pallas kernels for 0% -> 0%
where the time goes in v1:
time: 74.9 us; the launch traced here: 74.7 us
  Pallas kernels  70.9 us (95%)
  local copies, waits for them, and re-layouts  2.57 us (3%)
    pallas_call x1, Pallas kernels, per_device(): pl.pallas_call(functools.partial(kernel, planes, group_size, cap, lanes),...  70.9 us
    unnamed x5, local copies, waits for them, and re-layouts  1.88 us

profile of v1, /device:TPU:0, one launch (start us, length us, event | category | flops | bytes accessed | tf_op | source)
XLA Modules:
  0.0 74.7 jit_solution(7079273065466795592)
XLA Ops:
  0.6 0.0 copy-start.1
  0.6 0.7 reshape.10.clusters_ref
  1.3 0.0 copy-done.1
  1.3 0.0 copy-start
  1.3 1.1 %copy-done = bf16[384,768]{1,0:T(8,128)(2,1)S(1)} copy-done((bf16[384,768]{1,0:T(8,128)(2,1)S(1)}, bf16[384,768]{1,0:T(8,128)(2,1)}, u32[]{:S(2)}) %copy-start) | copy-done | bytes 589848
  2.4 70.9 %shard_map.50 = (bf16[384,768]{1,0:T(8,128)(2,1)S(1)}, f32[1,384]{1,0:T(1,128)S(1)}) custom-call(bf16[384,768]{1,0:T(8,128)(2,1)S(1)} %copy-done, s32[1,384]{1,0:T(1,128)S(1)} %reshape.10.clusters_ref, s32[16]{0:T(128)S(1)} %copy-done.1), custom_call_target="tpu_custom_call" | custom-call | tf_op jit(solution)/shard_map/pallas_call | solution.py:278
  73.3 0.6 reduce
  73.9 0.8 %copy.6 = bf16[384,768]{1,0:T(8,128)(2,1)} copy(bf16[384,768]{1,0:T(8,128)(2,1)S(1)} %get-tuple-element.8) | data formatting | bytes 1179648
Async XLA Ops:
  0.6 0.7 copy-start.1
  1.3 1.1 %copy-start = (bf16[384,768]{1,0:T(8,128)(2,1)S(1)}, bf16[384,768]{1,0:T(8,128)(2,1)}, u32[]{:S(2)}) copy-start(bf16[384,768]{1,0:T(8,128)(2,1)} %emb_ref.1) | copy-start | bytes 1769476

commit v2 on v1

--- a/solution.py
+++ b/solution.py
@@ -79,10 +79,6 @@
     slot_row = group_row * cap + rank_row
     slot_col = column(slot_row)
     cluster_col = column(clusters)
-    placing = (iota((planes * cap, rows), 0) == slot_row).astype(jnp.bfloat16)
-    placed = jnp.dot(placing, emb_ref[...], preferred_element_type=jnp.float32).astype(jnp.bfloat16)
-    outgoing[...] = placed.reshape(planes, cap, width)
-    keys[0, 0] = placed[:cap]
     for r in range(planes):
         lane = iota((rows, lanes), 1)
         here = (lane + r * cap == slot_col) & (lane < cap)
@@ -93,7 +89,7 @@
 
     pl.semaphore_wait(barrier, len(everyone) + planes - 1)
 
-    copies = []
+    copies, gone = [], []
 
     def send(src, dst, to):
         index = len(copies)
@@ -108,8 +104,18 @@
     half = (cap // 32 + (1 if cap % 32 else 0)) * 16
     lower, upper = pl.ds(0, half), pl.ds(half, cap - half)
 
+    def place(r):
+        placing = (iota((cap, rows), 0) + r * cap == slot_row).astype(jnp.bfloat16)
+        placed = jnp.dot(placing, emb_ref[...], preferred_element_type=jnp.float32)
+        return placed.astype(jnp.bfloat16)
+
     id_far = [None] + [send(out_ids.at[r], ids.at[0, r], far(r)) for r in range(1, planes)]
-    row_far = [None] + [send(outgoing.at[r], keys.at[r, 0], far(r)) for r in range(1, planes)]
+    row_far = [None]
+    for r in range(1, planes):
+        outgoing[r] = place(r)
+        if r < 3:
+            row_far.append(send(outgoing.at[r], keys.at[r, 0], far(r)))
+    keys[0, 0] = place(0)
 
     across, along = {}, {}
     last = {r: [] for r in range(planes)}
@@ -154,36 +160,10 @@
                 send(keys.at[r, member(ys - d, 0, 1)], keys.at[r, member(ys - d, 1, 1)], peer(0, 1, 0))
             )
 
-    own(0)
-    for r in range(1, planes):
-        id_far[r].wait_recv()
-    id_near = [
-        send(ids.at[0], ids.at[member((ys - dy) % ys, dc, ds)], peer(dy, dc, ds))
-        for dy, dc, ds in everyone
-    ]
-    for r in range(1, planes):
-        own(r)
-        forward(r - 1)
-        if r > 1:
-            share(r - 2)
-
     part = planes * cap // 2
-    for r in range(planes):
-        first = (planes - 1 - r) * cap
-        pick = iota((cap, lanes), 0) == iota((cap, lanes), 1)
-        query_ids[first:first + cap, :] = jnp.sum(
-            jnp.where(pick, ids[0, r], 0), axis=1, keepdims=True
-        )
-    acc[...] = jnp.zeros_like(acc)
-    peak[...] = jnp.zeros_like(peak)
-    total[...] = jnp.ones_like(total)
-    for copy in id_near:
-        copy.wait_recv()
 
     def step(r, h):
         start = h * part
-        if not isinstance(start, int):
-            start = pl.multiple_of(start, 16)
         mine = pl.ds(start, part)
         block = keys[r].reshape(members * cap, width)
         scores = lax.dot_general(
@@ -207,25 +187,55 @@
             weights.astype(jnp.bfloat16), block, preferred_element_type=jnp.float32
         )
 
-    def both(r):
-        def body(h, carry):
-            step(r, h)
-            return carry
-
-        lax.fori_loop(0, 2, body, 0)
-
     def finish(r):
         for copy in last[r]:
             copy.wait_recv()
 
-    for r in range(planes - 2):
-        finish(r)
-        both(r)
+    own(0)
+    for r in range(1, planes):
+        id_far[r].wait_recv()
+    id_near = [
+        send(ids.at[0], ids.at[member((ys - dy) % ys, dc, ds)], peer(dy, dc, ds))
+        for dy, dc, ds in everyone
+    ]
+    for r in range(planes):
+        first = (planes - 1 - r) * cap
+        pick = iota((cap, lanes), 0) == iota((cap, lanes), 1)
+        query_ids[first:first + cap, :] = jnp.sum(
+            jnp.where(pick, ids[0, r], 0), axis=1, keepdims=True
+        )
+    acc[...] = jnp.zeros_like(acc)
+    peak[...] = jnp.zeros_like(peak)
+    total[...] = jnp.ones_like(total)
+    near = planes // 2
+    waiting = []
+    for r in range(planes - 1):
+        forward(r)
+        own(r + 1)
+        if r + 3 < planes:
+            row_far[r + 2].wait_send()
+            gone.append(row_far[r + 2])
+            row_far.append(send(outgoing.at[r + 3], keys.at[r + 3, 0], far(r + 3)))
+        if r == 0:
+            for copy in id_near:
+                copy.wait_recv()
+        if r < planes - 2:
+            share(r)
+        if r + 1 >= near - 1 and r < planes - 2:
+            for k in range(len(waiting), r + 1):
+                finish(k)
+                step(k, 1)
+                waiting.append(k)
+    for k in waiting:
+        step(k, 0)
+    share(planes - 2)
     forward(planes - 1)
-    share(planes - 2)
-    finish(planes - 2)
-    both(planes - 2)
+    for k in range(len(waiting), planes - 1):
+        finish(k)
+        step(k, 1)
     share(planes - 1)
+    for k in range(len(waiting), planes - 1):
+        step(k, 0)
     finish(planes - 1)
 
     returned = []
@@ -258,7 +268,8 @@
         mass = mass + jnp.sum(jnp.where(here, back_mass[r], 0.0), axis=1, keepdims=True)
     mass_ref[...] = jnp.sum(jnp.where(eye, mass, 0.0), axis=0, keepdims=True)
     for copy in copies:
-        copy.wait_send()
+        if all(copy is not other for other in gone):
+            copy.wait_send()
 
 
 def per_device(embeddings, clusters, cluster_owner):

time: 74.9 us -> 74.9 us (level)
  no operation moved by 1% of the time
where the time goes in v2:
time: 74.9 us; the launch traced here: 74.7 us
  Pallas kernels  70.9 us (95%)
  local copies, waits for them, and re-layouts  2.57 us (3%)
    pallas_call x1, Pallas kernels, per_device(): pl.pallas_call(functools.partial(kernel, planes, group_size, cap, lanes),...  70.9 us
    unnamed x5, local copies, waits for them, and re-layouts  1.88 us

profile of v2, /device:TPU:0, one launch (start us, length us, event | category | flops | bytes accessed | tf_op | source)
XLA Modules:
  0.0 74.7 jit_solution(4596789558863506749)
XLA Ops:
  0.6 0.0 copy-start.1
  0.6 0.7 reshape.10.clusters_ref
  1.3 0.0 copy-done.1
  1.3 0.0 copy-start
  1.3 1.1 %copy-done = bf16[384,768]{1,0:T(8,128)(2,1)S(1)} copy-done((bf16[384,768]{1,0:T(8,128)(2,1)S(1)}, bf16[384,768]{1,0:T(8,128)(2,1)}, u32[]{:S(2)}) %copy-start) | copy-done | bytes 589848
  2.4 70.9 %shard_map.50 = (bf16[384,768]{1,0:T(8,128)(2,1)S(1)}, f32[1,384]{1,0:T(1,128)S(1)}) custom-call(bf16[384,768]{1,0:T(8,128)(2,1)S(1)} %copy-done, s32[1,384]{1,0:T(1,128)S(1)} %reshape.10.clusters_ref, s32[16]{0:T(128)S(1)} %copy-done.1), custom_call_target="tpu_custom_call" | custom-call | tf_op jit(solution)/shard_map/pallas_call | solution.py:289
  73.3 0.6 reduce
  73.9 0.8 %copy.6 = bf16[384,768]{1,0:T(8,128)(2,1)} copy(bf16[384,768]{1,0:T(8,128)(2,1)S(1)} %get-tuple-element.8) | data formatting | bytes 1179648
Async XLA Ops:
  0.6 0.7 copy-start.1
  1.3 1.1 %copy-start = (bf16[384,768]{1,0:T(8,128)(2,1)S(1)}, bf16[384,768]{1,0:T(8,128)(2,1)}, u32[]{:S(2)}) copy-start(bf16[384,768]{1,0:T(8,128)(2,1)} %emb_ref.1) | copy-start | bytes 1769476

commit v3 on v2

--- a/solution.py
+++ b/solution.py
@@ -24,9 +24,11 @@
 def kernel(
     planes, group_size, cap, lanes, emb_ref, clusters_ref, owner_ref, out_ref, mass_ref,
     keys, ids, queries, query_ids, acc, peak, total, outgoing, out_ids, results, masses, back, back_mass,
-    send_sem, recv_sem,
+    emb, load_sem, send_sem, recv_sem,
 ):
     rows, width = emb_ref.shape
+    load = pltpu.make_async_copy(emb_ref, emb, load_sem)
+    load.start()
     ys = group_size // 2
     members = group_size * SUB
     group_pos = lax.axis_index("group")
@@ -34,8 +36,13 @@
     my_y, my_core = group_pos // 2, group_pos % 2
     my_plane, my_sub = tile_pos // SUB, tile_pos % SUB
 
+    straight = [(dy, dc, ds) for dc in range(2) for dy in range(ys) for ds in range(SUB) if not (dy and ds)]
+    turning = [(dy, dc, ds) for dc in range(2) for dy in range(ys) for ds in range(SUB) if dy and ds]
+    places = straight + turning
+    early = len(straight)
+
     def member(dy, dc, ds):
-        return (dy * 2 + dc) * SUB + ds
+        return places.index((dy, dc, ds))
 
     def peer(dy, dc, ds):
         y = lax.rem(my_y + dy, ys)
@@ -63,7 +70,7 @@
     for r in range(1, planes):
         pl.semaphore_signal(barrier, inc=1, device_id=far(r), device_id_type=MESH)
 
-    clusters = clusters_ref[...]
+    clusters = clusters_ref[...].reshape(1, rows)
     group_row = jnp.zeros_like(clusters)
     for c in range(owner_ref.shape[0]):
         group_row = jnp.where(clusters == c, owner_ref[c], group_row)
@@ -79,14 +86,7 @@
     slot_row = group_row * cap + rank_row
     slot_col = column(slot_row)
     cluster_col = column(clusters)
-    for r in range(planes):
-        lane = iota((rows, lanes), 1)
-        here = (lane + r * cap == slot_col) & (lane < cap)
-        row = jnp.sum(jnp.where(here, cluster_col + 1, 0), axis=0, keepdims=True) - 1
-        out_ids[r] = row
-        if r == 0:
-            ids[0, 0] = row
-
+    load.wait()
     pl.semaphore_wait(barrier, len(everyone) + planes - 1)
 
     copies, gone = [], []
@@ -106,16 +106,8 @@
 
     def place(r):
         placing = (iota((cap, rows), 0) + r * cap == slot_row).astype(jnp.bfloat16)
-        placed = jnp.dot(placing, emb_ref[...], preferred_element_type=jnp.float32)
+        placed = jnp.dot(placing, emb[...], preferred_element_type=jnp.float32)
         return placed.astype(jnp.bfloat16)
-
-    id_far = [None] + [send(out_ids.at[r], ids.at[0, r], far(r)) for r in range(1, planes)]
-    row_far = [None]
-    for r in range(1, planes):
-        outgoing[r] = place(r)
-        if r < 3:
-            row_far.append(send(outgoing.at[r], keys.at[r, 0], far(r)))
-    keys[0, 0] = place(0)
 
     across, along = {}, {}
     last = {r: [] for r in range(planes)}
@@ -152,31 +144,37 @@
             last[r].append(send(side, keys.at[r, member(ys - d, 1, 0)], peer(0, 1, 0)))
         diagonal[r] = turned + crossed
 
+    tail = {r: [] for r in range(planes)}
+
     def share(r):
         for copy in diagonal[r]:
             copy.wait_recv()
         for d in range(1, ys):
-            last[r].append(
+            tail[r].append(
                 send(keys.at[r, member(ys - d, 0, 1)], keys.at[r, member(ys - d, 1, 1)], peer(0, 1, 0))
             )
 
-    part = planes * cap // 2
-
-    def step(r, h):
-        start = h * part
-        mine = pl.ds(start, part)
-        block = keys[r].reshape(members * cap, width)
+    def finish(copies_in):
+        for copy in copies_in:
+            copy.wait_recv()
+
+    def step(r, query_from, query_to, member_from=0, member_to=members):
+        start, size = query_from * cap, (query_to - query_from) * cap
+        mine = pl.ds(start, size)
+        block = keys[r, member_from:member_to].reshape((member_to - member_from) * cap, width)
         scores = lax.dot_general(
             queries[mine, :], block, (((1,), (1,)), ((), ())), preferred_element_type=jnp.float32
         )
-        key_ids = jnp.concatenate([ids[p, r][:, :cap] for p in range(members)], axis=1)
+        key_ids = jnp.concatenate([ids[p, r][:, :cap] for p in range(member_from, member_to)], axis=1)
         other = jnp.where(key_ids < 0, NEVER, -penalty * LOG2E)
         bias = jnp.where(query_ids[mine, :] == key_ids, 0.0, other)
         scores = scores * (score_scale * LOG2E / math.sqrt(width)) + bias
-        head = scores[:, :lanes]
-        lane = iota((part, lanes), 1)
-        itself = (iota((part, lanes), 0) - ((planes - 1 - r) * cap - start) == lane) & (lane < cap)
-        scores = jnp.concatenate([jnp.where(itself, NEVER, head), scores[:, lanes:]], axis=1)
+        spot = planes - 1 - r
+        if member_from == 0 and query_from <= spot < query_to:
+            head = scores[:, :lanes]
+            lane = iota((size, lanes), 1)
+            itself = (iota((size, lanes), 0) - (spot * cap - start) == lane) & (lane < cap)
+            scores = jnp.concatenate([jnp.where(itself, NEVER, head), scores[:, lanes:]], axis=1)
         old = peak[mine, :]
         new = jnp.maximum(old, jnp.max(scores, axis=1, keepdims=True))
         shrink = jnp.exp2(old - new)
@@ -187,13 +185,26 @@
             weights.astype(jnp.bfloat16), block, preferred_element_type=jnp.float32
         )
 
-    def finish(r):
-        for copy in last[r]:
-            copy.wait_recv()
-
+    keys[0, 0] = place(0)
     own(0)
+    row_far = [None]
     for r in range(1, planes):
-        id_far[r].wait_recv()
+        outgoing[r] = place(r)
+        if r < 3:
+            row_far.append(send(outgoing.at[r], keys.at[r, 0], far(r)))
+    for r in range(planes):
+        lane = iota((rows, lanes), 1)
+        here = (lane + r * cap == slot_col) & (lane < cap)
+        row = jnp.sum(jnp.where(here, cluster_col + 1, 0), axis=0, keepdims=True) - 1
+        out_ids[r] = row
+        if r == 0:
+            ids[0, 0] = row
+
+    id_far = [send(out_ids.at[r], ids.at[0, r], far(r)) for r in range(1, planes)]
+    acc[...] = jnp.zeros_like(acc)
+    peak[...] = jnp.zeros_like(peak)
+    total[...] = jnp.ones_like(total)
+    finish(id_far)
     id_near = [
         send(ids.at[0], ids.at[member((ys - dy) % ys, dc, ds)], peer(dy, dc, ds))
         for dy, dc, ds in everyone
@@ -204,12 +215,8 @@
         query_ids[first:first + cap, :] = jnp.sum(
             jnp.where(pick, ids[0, r], 0), axis=1, keepdims=True
         )
-    acc[...] = jnp.zeros_like(acc)
-    peak[...] = jnp.zeros_like(peak)
-    total[...] = jnp.ones_like(total)
-    near = planes // 2
-    waiting = []
-    for r in range(planes - 1):
+    final = planes - 1
+    for r in range(final):
         forward(r)
         own(r + 1)
         if r + 3 < planes:
@@ -217,56 +224,59 @@
             gone.append(row_far[r + 2])
             row_far.append(send(outgoing.at[r + 3], keys.at[r + 3, 0], far(r + 3)))
         if r == 0:
-            for copy in id_near:
-                copy.wait_recv()
-        if r < planes - 2:
+            finish(id_near)
+        if r + 1 < final - 1:
             share(r)
-        if r + 1 >= near - 1 and r < planes - 2:
-            for k in range(len(waiting), r + 1):
-                finish(k)
-                step(k, 1)
-                waiting.append(k)
-    for k in waiting:
-        step(k, 0)
-    share(planes - 2)
-    forward(planes - 1)
-    for k in range(len(waiting), planes - 1):
-        finish(k)
-        step(k, 1)
-    share(planes - 1)
-    for k in range(len(waiting), planes - 1):
-        step(k, 0)
-    finish(planes - 1)
-
-    returned = []
-    for h in range(2):
-        step(planes - 1, h)
-        for spot in range(h * planes // 2, (h + 1) * planes // 2):
-            r = planes - 1 - spot
-            first = spot * cap
-            sums = total[first:first + cap, :]
-            results[r] = (acc[first:first + cap, :] / sums).astype(jnp.bfloat16)
-            mass = peak[first:first + cap, :] * LN2 + jnp.log(sums)
-            pick = iota((cap, lanes), 0) == iota((cap, lanes), 1)
-            masses[r] = jnp.sum(jnp.where(pick, mass, 0.0), axis=0, keepdims=True)
-            if r:
-                returned.append(send(results.at[r], back.at[r], far(r)))
-                returned.append(send(masses.at[r], back_mass.at[r], far(r)))
-            else:
-                back[0] = results[0]
-                back_mass[0] = masses[0]
-    for copy in returned:
-        copy.wait_recv()
-
-    fetch = (iota((rows, planes * cap), 1) == slot_col).astype(jnp.bfloat16)
-    found = back[...].reshape(planes * cap, width)
-    out_ref[...] = jnp.dot(fetch, found, preferred_element_type=jnp.float32).astype(jnp.bfloat16)
+            finish(last[r] + tail[r])
+        elif r + 1 == final - 1:
+            for k in range(r):
+                step(k, 1, planes)
+            share(r)
+            finish(last[r] + tail[r])
+            step(r, 1, planes)
+    for k in range(final - 1):
+        step(k, 0, 1)
+    share(final - 1)
+    finish(last[final - 1] + tail[final - 1])
+    middle = planes // 2
+    step(final - 1, 0, middle)
+    forward(final)
+    step(final - 1, middle, planes)
+    finish(last[final])
+    step(final, middle, planes, 0, early)
+    share(final)
+    step(final, 0, middle, 0, early)
+    finish(tail[final])
+
+    returned = [None] * planes
+    for spot in range(planes):
+        step(final, spot, spot + 1, early, members)
+        r = final - spot
+        first = spot * cap
+        sums = total[first:first + cap, :]
+        results[r] = (acc[first:first + cap, :] / sums).astype(jnp.bfloat16)
+        mass = peak[first:first + cap, :] * LN2 + jnp.log(sums)
+        pick = iota((cap, lanes), 0) == iota((cap, lanes), 1)
+        masses[r] = jnp.sum(jnp.where(pick, mass, 0.0), axis=0, keepdims=True)
+        if r:
+            returned[r] = [
+                send(results.at[r], back.at[r], far(r)), send(masses.at[r], back_mass.at[r], far(r))
+            ]
+    found = jnp.zeros((rows, width), jnp.float32)
     mass = jnp.zeros((rows, 1), jnp.float32)
     for r in range(planes):
         lane = iota((rows, lanes), 1)
         here = (lane + r * cap == slot_col) & (lane < cap)
-        mass = mass + jnp.sum(jnp.where(here, back_mass[r], 0.0), axis=1, keepdims=True)
-    mass_ref[...] = jnp.sum(jnp.where(eye, mass, 0.0), axis=0, keepdims=True)
+        fetch = (iota((rows, cap), 1) + r * cap == slot_col).astype(jnp.bfloat16)
+        if r:
+            finish(returned[r])
+            block, block_mass = back[r], back_mass[r]
+        else:
+            block, block_mass = results[0], masses[0]
+        found = found + jnp.dot(fetch, block, preferred_element_type=jnp.float32)
+        mass = mass + jnp.sum(jnp.where(here, block_mass, 0.0), axis=1, keepdims=True)
+    out_ref[...] = found.astype(jnp.bfloat16)
+    mass_ref[...] = jnp.sum(jnp.where(eye, mass, 0.0), axis=0)
     for copy in copies:
         if all(copy is not other for other in gone):
             copy.wait_send()
@@ -290,9 +300,9 @@
         functools.partial(kernel, planes, group_size, cap, lanes),
         out_shape=(
             jax.ShapeDtypeStruct((rows, width), jnp.bfloat16),
-            jax.ShapeDtypeStruct((1, rows), jnp.float32),
+            jax.ShapeDtypeStruct((rows,), jnp.float32),
         ),
-        in_specs=[vmem, vmem, pl.BlockSpec(memory_space=pltpu.SMEM)],
+        in_specs=[pl.BlockSpec(memory_space=pl.ANY), vmem, pl.BlockSpec(memory_space=pltpu.SMEM)],
         out_specs=(vmem, vmem),
         scratch_shapes=[
             pltpu.VMEM((planes, members, cap, width), jnp.bfloat16),
@@ -308,14 +318,16 @@
             pltpu.VMEM((planes, 1, lanes), jnp.float32),
             pltpu.VMEM((planes, cap, width), jnp.bfloat16),
             pltpu.VMEM((planes, 1, lanes), jnp.float32),
+            pltpu.VMEM((rows, width), jnp.bfloat16),
+            pltpu.SemaphoreType.DMA,
             pltpu.SemaphoreType.DMA((count,)),
             pltpu.SemaphoreType.DMA((count,)),
         ],
         compiler_params=pltpu.CompilerParams(
-            collective_id=0, has_side_effects=True, vmem_limit_bytes=48 * 1024 * 1024
+            collective_id=0, has_side_effects=True, vmem_limit_bytes=63 * 1024 * 1024
         ),
-    )(embeddings, clusters.reshape(1, rows), cluster_owner)
-    return out, mass.reshape(rows)
+    )(embeddings, clusters, cluster_owner)
+    return out, mass
 
 
 def solution(mesh):

time: 74.9 us -> 79.2 us (1.057)
  Pallas kernels: 70.9 us -> 75.8 us
    pallas_call x1, Pallas kernels: 70.9 us -> 75.8 us  [per_device(): pl.pallas_call(functools.partial(kernel, planes, group_size, cap, lanes),...]
    unnamed x5 -> x4, local copies, waits for them, and re-layouts: 1.88 us -> 2.5 us
where the time goes in v3:
time: 79.2 us; the launch traced here: 79 us
  Pallas kernels  75.8 us (96%)
  local copies, waits for them, and re-layouts  2.5 us (3%)
    pallas_call x1, Pallas kernels, per_device(): pl.pallas_call(functools.partial(kernel, planes, group_size, cap, lanes),...  75.8 us
    unnamed x4, local copies, waits for them, and re-layouts  2.5 us

profile of v3, /device:TPU:0, one launch (start us, length us, event | category | flops | bytes accessed | tf_op | source)
XLA Modules:
  0.0 79.0 jit_solution(4322111378754381888)
XLA Ops:
  0.6 75.8 %shard_map.50 = (bf16[384,768]{1,0:T(8,128)(2,1)}, f32[384]{0:T(512)}) custom-call(bf16[384,768]{1,0:T(8,128)(2,1)} %emb_ref.1, s32[384]{0:T(512)} %clusters_ref.1, s32[16]{0:T(128)} %owner_ref.1), custom_call_target="tpu_custom_call" | custom-call | tf_op jit(solution)/shard_map/pallas_call | solution.py:299
  76.5 0.0 copy-start
  76.5 1.9 %copy.7 = bf16[384,768]{1,0:T(8,128)(2,1)} copy(bf16[384,768]{1,0:T(8,128)(2,1)} %get-tuple-element.4) | data formatting | bytes 1179648
  78.4 0.0 copy-done
  78.4 0.6 copy.8
Async XLA Ops:
  76.5 1.9 %copy-start = (f32[384]{0:T(512)S(1)}, f32[384]{0:T(512)}, u32[]{:S(2)}) copy-start(f32[384]{0:T(512)} %get-tuple-element.5) | copy-start | bytes 4612

commit v4 on v3

--- a/solution.py
+++ b/solution.py
@@ -24,11 +24,9 @@
 def kernel(
     planes, group_size, cap, lanes, emb_ref, clusters_ref, owner_ref, out_ref, mass_ref,
     keys, ids, queries, query_ids, acc, peak, total, outgoing, out_ids, results, masses, back, back_mass,
-    emb, load_sem, send_sem, recv_sem,
+    send_sem, recv_sem,
 ):
     rows, width = emb_ref.shape
-    load = pltpu.make_async_copy(emb_ref, emb, load_sem)
-    load.start()
     ys = group_size // 2
     members = group_size * SUB
     group_pos = lax.axis_index("group")
@@ -86,7 +84,6 @@
     slot_row = group_row * cap + rank_row
     slot_col = column(slot_row)
     cluster_col = column(clusters)
-    load.wait()
     pl.semaphore_wait(barrier, len(everyone) + planes - 1)
 
     copies, gone = [], []
@@ -106,7 +103,7 @@
 
     def place(r):
         placing = (iota((cap, rows), 0) + r * cap == slot_row).astype(jnp.bfloat16)
-        placed = jnp.dot(placing, emb[...], preferred_element_type=jnp.float32)
+        placed = jnp.dot(placing, emb_ref[...], preferred_element_type=jnp.float32)
         return placed.astype(jnp.bfloat16)
 
     across, along = {}, {}
@@ -215,42 +212,46 @@
         query_ids[first:first + cap, :] = jnp.sum(
             jnp.where(pick, ids[0, r], 0), axis=1, keepdims=True
         )
-    final = planes - 1
-    for r in range(final):
+    final, middle = planes - 1, planes // 2
+    scored = 0
+    for r in range(final - 1):
+        own(r + 1)
         forward(r)
-        own(r + 1)
         if r + 3 < planes:
             row_far[r + 2].wait_send()
             gone.append(row_far[r + 2])
             row_far.append(send(outgoing.at[r + 3], keys.at[r + 3, 0], far(r + 3)))
         if r == 0:
             finish(id_near)
-        if r + 1 < final - 1:
-            share(r)
-            finish(last[r] + tail[r])
-        elif r + 1 == final - 1:
-            for k in range(r):
-                step(k, 1, planes)
-            share(r)
-            finish(last[r] + tail[r])
-            step(r, 1, planes)
+            continue
+        share(r - 1)
+        if r + 1 >= middle:
+            for k in range(scored, r):
+                finish(last[k] + tail[k])
+                step(k, middle, planes)
+            scored = r
+    forward(final - 1)
+    share(final - 2)
+    finish(last[final - 2] + tail[final - 2])
+    step(final - 2, middle, planes)
+    own(final)
     for k in range(final - 1):
-        step(k, 0, 1)
-    share(final - 1)
+        step(k, 0, middle)
+        if k == 0:
+            share(final - 1)
+    forward(final)
     finish(last[final - 1] + tail[final - 1])
-    middle = planes // 2
+    step(final - 1, middle, planes)
+    share(final)
     step(final - 1, 0, middle)
-    forward(final)
-    step(final - 1, middle, planes)
-    finish(last[final])
-    step(final, middle, planes, 0, early)
-    share(final)
-    step(final, 0, middle, 0, early)
-    finish(tail[final])
+    finish(last[final] + tail[final])
 
     returned = [None] * planes
     for spot in range(planes):
-        step(final, spot, spot + 1, early, members)
+        if spot == 0:
+            step(final, 0, middle)
+        elif spot == middle:
+            step(final, middle, planes)
         r = final - spot
         first = spot * cap
         sums = total[first:first + cap, :]
@@ -302,7 +303,7 @@
             jax.ShapeDtypeStruct((rows, width), jnp.bfloat16),
             jax.ShapeDtypeStruct((rows,), jnp.float32),
         ),
-        in_specs=[pl.BlockSpec(memory_space=pl.ANY), vmem, pl.BlockSpec(memory_space=pltpu.SMEM)],
+        in_specs=[vmem, vmem, pl.BlockSpec(memory_space=pltpu.SMEM)],
         out_specs=(vmem, vmem),
         scratch_shapes=[
             pltpu.VMEM((planes, members, cap, width), jnp.bfloat16),
@@ -318,13 +319,11 @@
             pltpu.VMEM((planes, 1, lanes), jnp.float32),
             pltpu.VMEM((planes, cap, width), jnp.bfloat16),
             pltpu.VMEM((planes, 1, lanes), jnp.float32),
-            pltpu.VMEM((rows, width), jnp.bfloat16),
-            pltpu.SemaphoreType.DMA,
             pltpu.SemaphoreType.DMA((count,)),
             pltpu.SemaphoreType.DMA((count,)),
         ],
         compiler_params=pltpu.CompilerParams(
-            collective_id=0, has_side_effects=True, vmem_limit_bytes=63 * 1024 * 1024
+            collective_id=0, has_side_effects=True, vmem_limit_bytes=48 * 1024 * 1024
         ),
     )(embeddings, clusters, cluster_owner)
     return out, mass

time: 79.2 us -> 80.7 us (1.019)
  local copies, waits for them, and re-layouts: 2.5 us -> 3.79 us
    unnamed x4 -> x8, local copies, waits for them, and re-layouts: 2.5 us -> 3.79 us
where the time goes in v4:
time: 80.7 us; the launch traced here: 80.5 us
  Pallas kernels  76 us (94%)
  local copies, waits for them, and re-layouts  3.79 us (5%)
    pallas_call x1, Pallas kernels, per_device(): pl.pallas_call(functools.partial(kernel, planes, group_size, cap, lanes),...  76 us
    unnamed x8, local copies, waits for them, and re-layouts  3.79 us

profile of v4, /device:TPU:0, one launch (start us, length us, event | category | flops | bytes accessed | tf_op | source)
XLA Modules:
  0.0 80.5 jit_solution(14119104707103963042)
XLA Ops:
  0.6 0.0 copy-start
  0.6 1.1 %copy-done = bf16[384,768]{1,0:T(8,128)(2,1)S(1)} copy-done((bf16[384,768]{1,0:T(8,128)(2,1)S(1)}, bf16[384,768]{1,0:T(8,128)(2,1)}, u32[]{:S(2)}) %copy-start) | copy-done | bytes 589848
  1.7 0.0 copy-start.1
  1.7 0.7 copy-done.1
  2.4 0.0 copy-start.2
  2.4 0.7 copy-done.2
  3.0 76.0 %shard_map.50 = (bf16[384,768]{1,0:T(8,128)(2,1)S(1)}, f32[384]{0:T(512)S(1)}) custom-call(bf16[384,768]{1,0:T(8,128)(2,1)S(1)} %copy-done, s32[384]{0:T(512)S(1)} %copy-done.1, s32[16]{0:T(128)S(1)} %copy-done.2), custom_call_target="tpu_custom_call" | custom-call | tf_op jit(solution)/shard_map/pallas_call | solution.py:300
  79.1 0.8 %copy.7 = bf16[384,768]{1,0:T(8,128)(2,1)} copy(bf16[384,768]{1,0:T(8,128)(2,1)S(1)} %get-tuple-element.4) | data formatting | bytes 1179648
  79.9 0.6 copy.8
Async XLA Ops:
  0.6 1.1 %copy-start = (bf16[384,768]{1,0:T(8,128)(2,1)S(1)}, bf16[384,768]{1,0:T(8,128)(2,1)}, u32[]{:S(2)}) copy-start(bf16[384,768]{1,0:T(8,128)(2,1)} %emb_ref.1) | copy-start | bytes 1769476
  1.7 0.7 copy-start.1
  2.4 0.7 copy-start.2

commit v5 on v4

--- a/solution.py
+++ b/solution.py
@@ -68,7 +68,7 @@
     for r in range(1, planes):
         pl.semaphore_signal(barrier, inc=1, device_id=far(r), device_id_type=MESH)
 
-    clusters = clusters_ref[...].reshape(1, rows)
+    clusters = clusters_ref[...]
     group_row = jnp.zeros_like(clusters)
     for c in range(owner_ref.shape[0]):
         group_row = jnp.where(clusters == c, owner_ref[c], group_row)
@@ -86,7 +86,7 @@
     cluster_col = column(clusters)
     pl.semaphore_wait(barrier, len(everyone) + planes - 1)
 
-    copies, gone = [], []
+    copies = []
 
     def send(src, dst, to):
         index = len(copies)
@@ -182,13 +182,6 @@
             weights.astype(jnp.bfloat16), block, preferred_element_type=jnp.float32
         )
 
-    keys[0, 0] = place(0)
-    own(0)
-    row_far = [None]
-    for r in range(1, planes):
-        outgoing[r] = place(r)
-        if r < 3:
-            row_far.append(send(outgoing.at[r], keys.at[r, 0], far(r)))
     for r in range(planes):
         lane = iota((rows, lanes), 1)
         here = (lane + r * cap == slot_col) & (lane < cap)
@@ -198,6 +191,12 @@
             ids[0, 0] = row
 
     id_far = [send(out_ids.at[r], ids.at[0, r], far(r)) for r in range(1, planes)]
+    row_far = [None]
+    for r in range(1, planes):
+        outgoing[r] = place(r)
+        row_far.append(send(outgoing.at[r], keys.at[r, 0], far(r)))
+    keys[0, 0] = place(0)
+    own(0)
     acc[...] = jnp.zeros_like(acc)
     peak[...] = jnp.zeros_like(peak)
     total[...] = jnp.ones_like(total)
@@ -213,33 +212,26 @@
             jnp.where(pick, ids[0, r], 0), axis=1, keepdims=True
         )
     final, middle = planes - 1, planes // 2
-    scored = 0
-    for r in range(final - 1):
-        own(r + 1)
-        forward(r)
-        if r + 3 < planes:
-            row_far[r + 2].wait_send()
-            gone.append(row_far[r + 2])
-            row_far.append(send(outgoing.at[r + 3], keys.at[r + 3, 0], far(r + 3)))
-        if r == 0:
-            finish(id_near)
-            continue
-        share(r - 1)
-        if r + 1 >= middle:
-            for k in range(scored, r):
-                finish(last[k] + tail[k])
-                step(k, middle, planes)
-            scored = r
-    forward(final - 1)
-    share(final - 2)
-    finish(last[final - 2] + tail[final - 2])
-    step(final - 2, middle, planes)
-    own(final)
-    for k in range(final - 1):
+    forward(0)
+    own(1)
+    share(0)
+    finish(id_near)
+    for r in range(2, planes):
+        own(r)
+        forward(r - 1)
+        if r == middle:
+            finish(last[0] + tail[0])
+            step(0, middle, planes)
+        if r > 2:
+            share(r - 2)
+    step(0, 0, middle)
+    for k in range(1, final - 1):
+        finish(last[k] + tail[k])
+        step(k, middle, planes)
+        if k == 1:
+            forward(final)
         step(k, 0, middle)
-        if k == 0:
-            share(final - 1)
-    forward(final)
+    share(final - 1)
     finish(last[final - 1] + tail[final - 1])
     step(final - 1, middle, planes)
     share(final)
@@ -277,10 +269,9 @@
         found = found + jnp.dot(fetch, block, preferred_element_type=jnp.float32)
         mass = mass + jnp.sum(jnp.where(here, block_mass, 0.0), axis=1, keepdims=True)
     out_ref[...] = found.astype(jnp.bfloat16)
-    mass_ref[...] = jnp.sum(jnp.where(eye, mass, 0.0), axis=0)
+    mass_ref[...] = jnp.sum(jnp.where(eye, mass, 0.0), axis=0, keepdims=True)
     for copy in copies:
-        if all(copy is not other for other in gone):
-            copy.wait_send()
+        copy.wait_send()
 
 
 def per_device(embeddings, clusters, cluster_owner):
@@ -301,7 +292,7 @@
         functools.partial(kernel, planes, group_size, cap, lanes),
         out_shape=(
             jax.ShapeDtypeStruct((rows, width), jnp.bfloat16),
-            jax.ShapeDtypeStruct((rows,), jnp.float32),
+            jax.ShapeDtypeStruct((1, rows), jnp.float32),
         ),
         in_specs=[vmem, vmem, pl.BlockSpec(memory_space=pltpu.SMEM)],
         out_specs=(vmem, vmem),
@@ -325,8 +316,8 @@
         compiler_params=pltpu.CompilerParams(
             collective_id=0, has_side_effects=True, vmem_limit_bytes=48 * 1024 * 1024
         ),
-    )(embeddings, clusters, cluster_owner)
-    return out, mass
+    )(embeddings, clusters.reshape(1, rows), cluster_owner)
+    return out, mass.reshape(rows)
 
 
 def solution(mesh):

time: 80.7 us -> 71.4 us (0.88)
  Pallas kernels: 76 us -> 67.4 us
  local copies, waits for them, and re-layouts: 3.79 us -> 2.57 us
    pallas_call x1, Pallas kernels: 76 us -> 67.4 us  [per_device(): pl.pallas_call(functools.partial(kernel, planes, group_size, cap, lanes),...]
    unnamed x8 -> x5, local copies, waits for them, and re-layouts: 3.79 us -> 1.88 us
where the time goes in v5:
time: 71.4 us; the launch traced here: 71.3 us
  Pallas kernels  67.4 us (94%)
  local copies, waits for them, and re-layouts  2.57 us (4%)
    pallas_call x1, Pallas kernels, per_device(): pl.pallas_call(functools.partial(kernel, planes, group_size, cap, lanes),...  67.4 us
    unnamed x5, local copies, waits for them, and re-layouts  1.88 us

profile of v5, /device:TPU:0, one launch (start us, length us, event | category | flops | bytes accessed | tf_op | source)
XLA Modules:
  0.0 71.3 jit_solution(2368236267007351915)
XLA Ops:
  0.6 0.0 copy-start.1
  0.6 0.7 reshape.10.clusters_ref
  1.3 0.0 copy-done.1
  1.3 0.0 copy-start
  1.3 1.1 %copy-done = bf16[384,768]{1,0:T(8,128)(2,1)S(1)} copy-done((bf16[384,768]{1,0:T(8,128)(2,1)S(1)}, bf16[384,768]{1,0:T(8,128)(2,1)}, u32[]{:S(2)}) %copy-start) | copy-done | bytes 589848
  2.4 67.4 %shard_map.50 = (bf16[384,768]{1,0:T(8,128)(2,1)S(1)}, f32[1,384]{1,0:T(1,128)S(1)}) custom-call(bf16[384,768]{1,0:T(8,128)(2,1)S(1)} %copy-done, s32[1,384]{1,0:T(1,128)S(1)} %reshape.10.clusters_ref, s32[16]{0:T(128)S(1)} %copy-done.1), custom_call_target="tpu_custom_call" | custom-call | tf_op jit(solution)/shard_map/pallas_call | solution.py:291
  69.8 0.6 reduce
  70.4 0.8 %copy.6 = bf16[384,768]{1,0:T(8,128)(2,1)} copy(bf16[384,768]{1,0:T(8,128)(2,1)S(1)} %get-tuple-element.8) | data formatting | bytes 1179648
Async XLA Ops:
  0.6 0.7 copy-start.1
  1.3 1.1 %copy-start = (bf16[384,768]{1,0:T(8,128)(2,1)S(1)}, bf16[384,768]{1,0:T(8,128)(2,1)}, u32[]{:S(2)}) copy-start(bf16[384,768]{1,0:T(8,128)(2,1)} %emb_ref.1) | copy-start | bytes 1769476

commit v6 on v5

--- a/solution.py
+++ b/solution.py
@@ -191,10 +191,10 @@
             ids[0, 0] = row
 
     id_far = [send(out_ids.at[r], ids.at[0, r], far(r)) for r in range(1, planes)]
-    row_far = [None]
-    for r in range(1, planes):
+    row_far = [None] * planes
+    for r in [*range(2, planes), 1]:
         outgoing[r] = place(r)
-        row_far.append(send(outgoing.at[r], keys.at[r, 0], far(r)))
+        row_far[r] = send(outgoing.at[r], keys.at[r, 0], far(r))
     keys[0, 0] = place(0)
     own(0)
     acc[...] = jnp.zeros_like(acc)

time: 71.4 us -> 76.6 us (1.073)
  Pallas kernels: 67.4 us -> 72.6 us
    pallas_call x1, Pallas kernels: 67.4 us -> 72.6 us  [per_device(): pl.pallas_call(functools.partial(kernel, planes, group_size, cap, lanes),...]
where the time goes in v6:
time: 76.6 us; the launch traced here: 76.4 us
  Pallas kernels  72.6 us (95%)
  local copies, waits for them, and re-layouts  2.57 us (3%)
    pallas_call x1, Pallas kernels, per_device(): pl.pallas_call(functools.partial(kernel, planes, group_size, cap, lanes),...  72.6 us
    unnamed x5, local copies, waits for them, and re-layouts  1.88 us

profile of v6, /device:TPU:0, one launch (start us, length us, event | category | flops | bytes accessed | tf_op | source)
XLA Modules:
  0.0 76.4 jit_solution(2944571707732014674)
XLA Ops:
  0.6 0.0 copy-start.1
  0.6 0.7 reshape.10.clusters_ref
  1.3 0.0 copy-done.1
  1.3 0.0 copy-start
  1.3 1.1 %copy-done = bf16[384,768]{1,0:T(8,128)(2,1)S(1)} copy-done((bf16[384,768]{1,0:T(8,128)(2,1)S(1)}, bf16[384,768]{1,0:T(8,128)(2,1)}, u32[]{:S(2)}) %copy-start) | copy-done | bytes 589848
  2.4 72.6 %shard_map.50 = (bf16[384,768]{1,0:T(8,128)(2,1)S(1)}, f32[1,384]{1,0:T(1,128)S(1)}) custom-call(bf16[384,768]{1,0:T(8,128)(2,1)S(1)} %copy-done, s32[1,384]{1,0:T(1,128)S(1)} %reshape.10.clusters_ref, s32[16]{0:T(128)S(1)} %copy-done.1), custom_call_target="tpu_custom_call" | custom-call | tf_op jit(solution)/shard_map/pallas_call | solution.py:291
  75.0 0.6 reduce
  75.6 0.8 %copy.6 = bf16[384,768]{1,0:T(8,128)(2,1)} copy(bf16[384,768]{1,0:T(8,128)(2,1)S(1)} %get-tuple-element.8) | data formatting | bytes 1179648
Async XLA Ops:
  0.6 0.7 copy-start.1
  1.3 1.1 %copy-start = (bf16[384,768]{1,0:T(8,128)(2,1)S(1)}, bf16[384,768]{1,0:T(8,128)(2,1)}, u32[]{:S(2)}) copy-start(bf16[384,768]{1,0:T(8,128)(2,1)} %emb_ref.1) | copy-start | bytes 1769476
